TPU v7x, 32 devices: a whole 2x2x4 slice. The times are simulated.
32 devices in a mesh: aux: 2 (over core), pair: 16 (over z, y, x).
Axes of the slice: x: 2, y: 2, z: 4, core: 2. Of those that a mesh axis runs over, the one named last changes fastest.
Arguments:
- metric_factor: bfloat16 [16384, 16384], P('pair', 'aux'), as said below
- three_centre: bfloat16 [16384, 1536], P('aux', 'pair')
- occ_energy: float32 [2], replicated, may hold values from -2 to -0.3
- virt_energy: float32 [768], replicated, may hold values from 0.2 to 3
Outputs:
- amplitudes: float32 [1536, 1536], P('pair', 'aux')
- energy: float32 [], replicated
Inputs may be any that keep to these rules, and one draw needn't show every extreme that they name: metric_factor is lower triangular: every entry above the diagonal is zero, and its diagonal lies between 0.5 and 1.5.
All inputs are finite; a program needn't handle non-finite values.
Results may differ from a plain program's by a relative error of at most 0.0023.
Values may be sent and summed in bfloat16 or wider, within the bound.
No kernel may reach another device: no remote copies, remote signals or barrier semaphores. Data moves between devices by JAX's collectives and lax.ppermute only.
A program may use at most 128 MiB of HBM per device.

v0:
```python
import jax
import jax.numpy as jnp
from jax import lax
from jax.sharding import PartitionSpec as P


def shards(metric_factor, three_centre, occ_energy, virt_energy):
    aux_count = lax.axis_size("aux")
    pair_count = lax.axis_size("pair")
    aux_id = lax.axis_index("aux")
    pair_id = lax.axis_index("pair")
    pairs_total = three_centre.shape[1] * pair_count
    share_cols = pairs_total // aux_count
    share_rows = pairs_total // pair_count
    partial_fit = jnp.dot(
        metric_factor,
        lax.all_gather(three_centre, "pair", axis=1, tiled=True),
        preferred_element_type=jnp.float32,
    )
    own_share = lax.psum_scatter(partial_fit, "aux", scatter_dimension=1, tiled=True).astype(
        jnp.bfloat16
    )
    fitted = lax.all_gather(own_share, "aux", axis=1, tiled=True)
    integrals = lax.psum_scatter(
        lax.dot_general(
            fitted, own_share, (((0,), (0,)), ((), ())), preferred_element_type=jnp.float32
        ),
        "pair",
        scatter_dimension=0,
        tiled=True,
    )
    pair_gap = (virt_energy[None, :] - occ_energy[:, None]).reshape(-1)
    row_gap = lax.dynamic_slice_in_dim(pair_gap, pair_id * share_rows, share_rows, 0)
    col_gap = lax.dynamic_slice_in_dim(pair_gap, aux_id * share_cols, share_cols, 0)
    denominator = row_gap[:, None] + col_gap[None, :]
    amplitudes = integrals / denominator
    local_energy = jnp.sum(integrals * amplitudes)
    energy = -lax.psum(local_energy, ("aux", "pair"))
    return (amplitudes, energy)


def solution(mesh):
    in_specs = (P("pair", "aux"), P("aux", "pair"), P(), P())
    out_specs = (P("pair", "aux"), P())
    return jax.shard_map(shards, mesh=mesh, in_specs=in_specs, out_specs=out_specs, check_vma=False)
```

profile of v0, /device:TPU:0, one launch (start us, length us, event | category | flops | bytes accessed | tf_op | source)
XLA Modules:
  0.0 544.9 jit_solution(17345936549371796398)
XLA Ops:
  7.2 0.0 all-gather.3.cloned.1.call-start
  7.2 0.7 all-gather.3.cloned.1.call-update
  7.9 0.0 reduce-scatter.3.cloned.1.call-start
  7.9 276.8 %all-gather.3.cloned.1.call-done = bf16[8192,1536]{0,1:T(8,128)(2,1)} async-done(((bf16[8192,96]{0,1:T(8,128)(2,1)}), bf16[8192,1536]{0,1:T(8,128)(2,1)}) %all-gather.3.cloned.1.call-update) | async-done | bytes 25165840 | tf_op jit(solution)/shard_map/all_gather | solution.py:17
  284.7 33.6 %fusion = f32[1024,1536]{1,0:T(8,128)} fusion(bf16[1024,8192]{1,0:T(8,128)(2,1)} %param.4, bf16[8192,1536]{0,1:T(8,128)(2,1)} %all-gather.3.cloned.1.call-done), kind=kOutput, calls=%fused_computation.3 | convolution fusion | flops 25769803776 | bytes 48234496 | tf_op jit(solution)/shard_map/dot_general | solution.py:15
  318.4 0.0 reduce-scatter.3.cloned.1.call-update
  318.4 0.0 all-gather.5.cloned.1.call-start
  318.4 12.8 %reduce-scatter.3.cloned.1.call-done = f32[1024,768]{1,0:T(8,128)} async-done(((f32[1024,1536]{1,0:T(8,128)}), f32[1024,768]{1,0:T(8,128)}) %reduce-scatter.3.cloned.1.call-update) | async-done | bytes 3145744 | tf_op jit(solution)/shard_map/reduce_scatter | solution.py:20
  331.3 3.3 convert_element_type.3
  334.5 0.0 all-gather.5.cloned.1.call-update
  334.6 0.0 reduce-scatter.5.cloned.1.call-start
  334.6 13.4 %all-gather.5.cloned.1.call-done = bf16[1024,1536]{1,0:T(8,128)(2,1)} async-done(((bf16[1024,768]{1,0:T(8,128)(2,1)}), bf16[1024,1536]{1,0:T(8,128)(2,1)}) %all-gather.5.cloned.1.call-update) | async-done | bytes 3145744 | tf_op jit(solution)/shard_map/all_gather | solution.py:23
  348.0 7.1 %fusion.1 = f32[1536,768]{1,0:T(8,128)} fusion(bf16[1024,1536]{1,0:T(8,128)(2,1)} %all-gather.5.cloned.1.call-done, bf16[1024,768]{1,0:T(8,128)(2,1)} %convert_element_type.3), kind=kOutput, calls=%fused_computation.4 | convolution fusion | flops 2415919104 | bytes 9437184 | tf_op jit(solution)/shard_map/dot_general | solution.py:25
  355.1 0.0 copy-start
  355.1 0.0 copy-start.1
  355.1 0.0 reduce-scatter.5.cloned.1.call-update
  355.2 0.7 copy-done
  355.8 0.0 copy-done.1
  355.8 0.1 broadcast_subtract_fusion
  355.9 0.1 dynamic_slice.7
  356.0 0.1 dynamic_slice.6
  356.1 138.1 %reduce-scatter.5.cloned.1.call-done = f32[96,768]{1,0:T(8,128)} async-done(((f32[1536,768]{1,0:T(8,128)}), f32[96,768]{1,0:T(8,128)}) %reduce-scatter.5.cloned.1.call-update) | async-done | bytes 294928 | tf_op jit(solution)/shard_map/reduce_scatter | solution.py:24
  494.1 2.4 multiply_reduce_fusion
  496.5 40.0 %psum.7 = f32[]{:T(128)} all-reduce(f32[]{:T(128)} %get-tuple-element.2), channel_id=1, replica_groups=mesh['aux'=2,'pair'=16] {'aux','pair'}, use_global_device_ids=true, to_apply=%region_3.0 | all-reduce | flops 1 | bytes 8 | tf_op jit(solution)/shard_map/psum | solution.py:38
  (1 shorter events, 0.0 us)
Async XLA Ops:
  7.2 277.6 %all-gather.3.cloned.1.call-start = ((), (), s32[]{:S(2)}) async-start(), calls=%async_computation.2 | async-start | bytes 26738688 | tf_op jit(solution)/shard_map/all_gather | solution.py:17
  7.9 323.4 %reduce-scatter.3.cloned.1.call-start = ((), (), s32[]{:S(2)}) async-start(), calls=%async_computation.3 | async-start | bytes 9437184 | tf_op jit(solution)/shard_map/reduce_scatter | solution.py:20
  318.4 29.6 %all-gather.5.cloned.1.call-start = ((), (), s32[]{:S(2)}) async-start(), calls=%async_computation.4 | async-start | bytes 4718592 | tf_op jit(solution)/shard_map/all_gather | solution.py:23
  334.6 159.6 %reduce-scatter.5.cloned.1.call-start = ((), (), s32[]{:S(2)}) async-start(), calls=%async_computation.5 | async-start | bytes 5013504 | tf_op jit(solution)/shard_map/reduce_scatter | solution.py:24
  355.1 0.7 copy-start
  355.1 0.7 copy-start.1
Sparse Core Ops, SparseCore 0:
  10.8 273.9 all-gather.2
  318.5 12.7 reduce-scatter.2
  334.7 13.2 all-gather.4
  355.3 138.7 reduce-scatter.4
where the time goes:
time: 545 us
  waiting for transfers between devices  442 us (81%)
  matrix products  40.8 us (7%)
  blocking collectives  40 us (7%)
  between operations  15.6 us (3%)
  other arithmetic  5.73 us (1%)
    all_gather x1, waiting for transfers between devices, shards(): lax.all_gather(three_centre, 'pair', axis=1, tiled=True)  277 us
    reduce_scatter x1, waiting for transfers between devices, shards(): lax.psum_scatter(lax.dot_general(fitted, own_share, (((0,), (0,)), ((), (...  138 us
    psum x1, blocking collectives, shards(): energy = -lax.psum(local_energy, ('aux', 'pair'))  40 us
    dot_general x1, matrix products, shards(): jnp.dot(metric_factor, lax.all_gather(three_centre, 'pair', axis=1, tiled...  33.6 us
    all_gather x1, waiting for transfers between devices, shards(): fitted = lax.all_gather(own_share, 'aux', axis=1, tiled=True)  13.4 us
    reduce_scatter x1, waiting for transfers between devices, shards(): lax.psum_scatter(partial_fit, 'aux', scatter_dimension=1, tiled=True)  12.8 us
  transfers between devices with their start and end apart: 4, of which 4 were waited for; matrix products, arithmetic and copies ran while one was open for 0% of the time, Pallas kernels for 0%

commit v1 on v0

--- a/solution.py
+++ b/solution.py
@@ -2,6 +2,12 @@
 import jax.numpy as jnp
 from jax import lax
 from jax.sharding import PartitionSpec as P
+
+
+def total_of(value, axes):
+    count = lax.axis_size(axes)
+    sent = jnp.broadcast_to(value, (count, 8, 128))
+    return jnp.sum(lax.all_to_all(sent, axes, 0, 0, tiled=True)[:, 0, 0])
 
 
 def shards(metric_factor, three_centre, occ_energy, virt_energy):
@@ -21,21 +27,19 @@
         jnp.bfloat16
     )
     fitted = lax.all_gather(own_share, "aux", axis=1, tiled=True)
-    integrals = lax.psum_scatter(
-        lax.dot_general(
-            fitted, own_share, (((0,), (0,)), ((), ())), preferred_element_type=jnp.float32
-        ),
-        "pair",
-        scatter_dimension=0,
-        tiled=True,
+    partial_tiles = lax.dot_general(
+        fitted, own_share, (((0,), (0,)), ((), ())), preferred_element_type=jnp.float32
+    ).astype(jnp.bfloat16)
+    tiles = lax.all_to_all(partial_tiles, "pair", 0, 0, tiled=True)
+    integrals = jnp.sum(
+        tiles.reshape(pair_count, share_rows, share_cols).astype(jnp.float32), axis=0
     )
     pair_gap = (virt_energy[None, :] - occ_energy[:, None]).reshape(-1)
     row_gap = lax.dynamic_slice_in_dim(pair_gap, pair_id * share_rows, share_rows, 0)
     col_gap = lax.dynamic_slice_in_dim(pair_gap, aux_id * share_cols, share_cols, 0)
     denominator = row_gap[:, None] + col_gap[None, :]
     amplitudes = integrals / denominator
-    local_energy = jnp.sum(integrals * amplitudes)
-    energy = -lax.psum(local_energy, ("aux", "pair"))
+    energy = -total_of(jnp.sum(integrals * amplitudes), ("aux", "pair"))
     return (amplitudes, energy)
 
 

time: 545 us -> 439 us (0.81)
  waiting for transfers between devices: 442 us -> 351 us
  blocking collectives: 40 us -> 18.6 us
  starting transfers between devices: 0.16 us -> 7.03 us
    reduce_scatter x1 -> x0, waiting for transfers between devices: 138 us -> none  [shards(): lax.psum_scatter(lax.dot_general(fitted, own_share, (((0,), (0,)), ((), (...]
    all_to_all x0 -> x1, waiting for transfers between devices: none -> 47.4 us  [shards(): tiles = lax.all_to_all(partial_tiles, 'pair', 0, 0, tiled=True)]
    psum x1 -> x0, blocking collectives: 40 us -> none  [shards(): energy = -lax.psum(local_energy, ('aux', 'pair'))]
    all_to_all x0 -> x1, blocking collectives: none -> 18.6 us  [total_of(): return jnp.sum(lax.all_to_all(sent, axes, 0, 0, tiled=True)[:, 0, 0])]
    all_to_all x0 -> x1, starting transfers between devices: none -> 6.92 us  [shards(): tiles = lax.all_to_all(partial_tiles, 'pair', 0, 0, tiled=True)]
where the time goes in v1:
time: 439 us
  waiting for transfers between devices  351 us (80%)
  matrix products  40.1 us (9%)
  blocking collectives  18.6 us (4%)
  between operations  15.6 us (4%)
  starting transfers between devices  7.03 us (2%)
  other arithmetic  5.66 us (1%)
    all_gather x1, waiting for transfers between devices, shards(): lax.all_gather(three_centre, 'pair', axis=1, tiled=True)  277 us
    all_to_all x1, waiting for transfers between devices, shards(): tiles = lax.all_to_all(partial_tiles, 'pair', 0, 0, tiled=True)  47.4 us
    dot_general x1, matrix products, shards(): jnp.dot(metric_factor, lax.all_gather(three_centre, 'pair', axis=1, tiled...  33.6 us
    all_to_all x1, blocking collectives, total_of(): return jnp.sum(lax.all_to_all(sent, axes, 0, 0, tiled=True)[:, 0, 0])  18.6 us
    all_gather x1, waiting for transfers between devices, shards(): fitted = lax.all_gather(own_share, 'aux', axis=1, tiled=True)  13.4 us
    reduce_scatter x1, waiting for transfers between devices, shards(): lax.psum_scatter(partial_fit, 'aux', scatter_dimension=1, tiled=True)  12.8 us
  transfers between devices with their start and end apart: 4, of which 4 were waited for; matrix products, arithmetic and copies ran while one was open for 0% of the time, Pallas kernels for 0%

profile of v1, /device:TPU:0, one launch (start us, length us, event | category | flops | bytes accessed | tf_op | source)
XLA Modules:
  0.0 438.9 jit_solution(10530660893675494034)
XLA Ops:
  7.2 0.0 all-gather.3.cloned.1.call-start
  7.2 0.7 all-gather.3.cloned.1.call-update
  7.9 0.0 reduce-scatter.2.cloned.1.call-start
  7.9 276.8 %all-gather.3.cloned.1.call-done = bf16[8192,1536]{0,1:T(8,128)(2,1)} async-done(((bf16[8192,96]{0,1:T(8,128)(2,1)}), bf16[8192,1536]{0,1:T(8,128)(2,1)}) %all-gather.3.cloned.1.call-update) | async-done | bytes 25165840 | tf_op jit(solution)/shard_map/all_gather | solution.py:23
  284.7 33.6 %fusion = f32[1024,1536]{1,0:T(8,128)} fusion(bf16[1024,8192]{1,0:T(8,128)(2,1)} %param.4, bf16[8192,1536]{0,1:T(8,128)(2,1)} %all-gather.3.cloned.1.call-done), kind=kOutput, calls=%fused_computation.6 | convolution fusion | flops 25769803776 | bytes 48234496 | tf_op jit(solution)/shard_map/dot_general | solution.py:21
  318.4 0.0 reduce-scatter.2.cloned.1.call-update
  318.4 0.0 all-gather.5.cloned.1.call-start
  318.5 12.8 %reduce-scatter.2.cloned.1.call-done = f32[1024,768]{1,0:T(8,128)} async-done(((f32[1024,1536]{1,0:T(8,128)}), f32[1024,768]{1,0:T(8,128)}) %reduce-scatter.2.cloned.1.call-update) | async-done | bytes 3145744 | tf_op jit(solution)/shard_map/reduce_scatter | solution.py:26
  331.3 3.2 convert_element_type.9
  334.5 0.0 all-gather.5.cloned.1.call-update
  334.5 13.4 %all-gather.5.cloned.1.call-done = bf16[1024,1536]{1,0:T(8,128)(2,1)} async-done(((bf16[1024,768]{1,0:T(8,128)(2,1)}), bf16[1024,1536]{1,0:T(8,128)(2,1)}) %all-gather.5.cloned.1.call-update) | async-done | bytes 3145744 | tf_op jit(solution)/shard_map/all_gather | solution.py:29
  347.9 6.5 %convolution_convert_fusion = bf16[1536,768]{1,0:T(8,128)(2,1)} fusion(bf16[1024,1536]{1,0:T(8,128)(2,1)} %all-gather.5.cloned.1.call-done, bf16[1024,768]{1,0:T(8,128)(2,1)} %convert_element_type.9), kind=kOutput, calls=%fused_computation.1 | convolution fusion | flops 2417098752 | bytes 7077888 | tf_op jit(solution)/shard_map/dot_general | solution.py:30
  354.4 0.0 copy-start
  354.4 0.0 copy-start.1
  354.4 6.9 %all-to-all-start = ((bf16[16,96,768]{2,1,0:T(8,128)(2,1)}), bf16[16,96,768]{2,1,0:T(8,128)(2,1)S(1)}, u32[]{:S(2)}, u32[]{:S(2)}) async-start(bf16[16,96,768]{2,1,0:T(8,128)(2,1)} %bitcast.5), calls=%async_computation.1 | async-start | bytes 4718592 | tf_op jit(solution)/shard_map/all_to_all | solution.py:33
  361.3 0.0 copy-done
  361.4 0.0 copy-done.1
  361.4 0.1 broadcast_subtract_fusion
  361.4 0.1 dynamic_slice.7
  361.5 0.1 dynamic_slice.6
  361.6 47.4 %all-to-all-done = bf16[16,96,768]{2,1,0:T(8,128)(2,1)S(1)} async-done(((bf16[16,96,768]{2,1,0:T(8,128)(2,1)}), bf16[16,96,768]{2,1,0:T(8,128)(2,1)S(1)}, u32[]{:S(2)}, u32[]{:S(2)}) %all-to-all-start) | async-done | bytes 2359328 | tf_op jit(solution)/shard_map/all_to_all | solution.py:33
  409.0 0.3 convert_reduce_fusion
  409.3 1.4 multiply_reduce_fusion
  410.7 0.7 broadcast_in_dim.2
  411.4 18.6 %all_to_all.14 = f32[32,8,128]{2,1,0:T(8,128)S(1)} all-to-all(f32[32,8,128]{2,1,0:T(8,128)S(1)} %broadcast_in_dim.2), channel_id=1, replica_groups=mesh['aux'=2,'pair'=16] {'aux','pair'}, dimensions={0} | all-to-all | bytes 262144 | tf_op jit(solution)/shard_map/all_to_all | solution.py:10
  430.0 0.6 slice_reduce_fusion
  (1 shorter events, 0.0 us)
Async XLA Ops:
  7.2 277.6 %all-gather.3.cloned.1.call-start = ((), (), s32[]{:S(2)}) async-start(), calls=%async_computation.3 | async-start | bytes 26738688 | tf_op jit(solution)/shard_map/all_gather | solution.py:23
  7.9 323.4 %reduce-scatter.2.cloned.1.call-start = ((), (), s32[]{:S(2)}) async-start(), calls=%async_computation.4 | async-start | bytes 9437184 | tf_op jit(solution)/shard_map/reduce_scatter | solution.py:26
  318.4 29.5 %all-gather.5.cloned.1.call-start = ((), (), s32[]{:S(2)}) async-start(), calls=%async_computation.5 | async-start | bytes 4718592 | tf_op jit(solution)/shard_map/all_gather | solution.py:29
  354.4 6.9 %copy-start = (f32[768]{0:T(1024)S(1)}, f32[768]{0:T(1024)}, u32[]{:S(2)}) copy-start(f32[768]{0:T(1024)} %param.7) | copy-start | bytes 9220
  354.4 6.9 %copy-start.1 = (f32[2]{0:T(128)S(1)}, f32[2]{0:T(128)}, u32[]{:S(2)}) copy-start(f32[2]{0:T(128)} %param.6) | copy-start | bytes 28
  354.4 54.6 %all-to-all-start = ((bf16[16,96,768]{2,1,0:T(8,128)(2,1)}), bf16[16,96,768]{2,1,0:T(8,128)(2,1)S(1)}, u32[]{:S(2)}, u32[]{:S(2)}) async-start(bf16[16,96,768]{2,1,0:T(8,128)(2,1)} %bitcast.5), calls=%async_computation.1 | async-start | bytes 4718592 | tf_op jit(solution)/shard_map/all_to_all | solution.py:33
Sparse Core Ops, SparseCore 0:
  10.8 273.9 all-gather.2
  318.5 12.7 reduce-scatter.1
  334.6 13.2 all-gather.4

commit v2 on v1

v2 whole, which is shorter than its diff:
```python
import functools

import jax
import jax.numpy as jnp
from jax import lax
from jax.experimental import pallas as pl
from jax.experimental.pallas import tpu as pltpu
from jax.sharding import PartitionSpec as P

AXES = ("aux", "pair")
LAYERS = 4
PLANE = 4
TURN = (1, 2)


def total_of(value, axes):
    count = lax.axis_size(axes)
    sent = jnp.broadcast_to(value, (count, 8, 128))
    return jnp.sum(lax.all_to_all(sent, axes, 0, 0, tiled=True)[:, 0, 0])


def nt_dot(left, right):
    return lax.dot_general(
        left, right, (((1,), (1,)), ((), ())), preferred_element_type=jnp.float32
    )


def outputs(tiles, occ_energy, virt_energy):
    pair_count, share_rows, share_cols = tiles.shape
    aux_id = lax.axis_index("aux")
    pair_id = lax.axis_index("pair")
    integrals = jnp.sum(tiles.astype(jnp.float32), axis=0)
    pair_gap = (virt_energy[None, :] - occ_energy[:, None]).reshape(-1)
    row_gap = lax.dynamic_slice_in_dim(pair_gap, pair_id * share_rows, share_rows, 0)
    col_gap = lax.dynamic_slice_in_dim(pair_gap, aux_id * share_cols, share_cols, 0)
    denominator = row_gap[:, None] + col_gap[None, :]
    amplitudes = integrals / denominator
    energy = -total_of(jnp.sum(integrals * amplitudes), AXES)
    return (amplitudes, energy)


def shards_any(metric_factor, three_centre, occ_energy, virt_energy):
    aux_count = lax.axis_size("aux")
    pair_count = lax.axis_size("pair")
    pairs_total = three_centre.shape[1] * pair_count
    share_cols = pairs_total // aux_count
    share_rows = pairs_total // pair_count
    partial_fit = jnp.dot(
        metric_factor,
        lax.all_gather(three_centre, "pair", axis=1, tiled=True),
        preferred_element_type=jnp.float32,
    )
    own_share = lax.psum_scatter(partial_fit, "aux", scatter_dimension=1, tiled=True).astype(
        jnp.bfloat16
    )
    fitted = lax.all_gather(own_share, "aux", axis=1, tiled=True)
    partial_tiles = lax.dot_general(
        fitted, own_share, (((0,), (0,)), ((), ())), preferred_element_type=jnp.float32
    ).astype(jnp.bfloat16)
    tiles = lax.all_to_all(partial_tiles, "pair", 0, 0, tiled=True)
    return outputs(tiles.reshape(pair_count, share_rows, share_cols), occ_energy, virt_energy)


def layers_of(core):
    return range(0, LAYERS) if core == 0 else range(LAYERS // 2, LAYERS)


def along(turn):
    pairs = []
    for core in range(2):
        for z in layers_of(core):
            at = (core * LAYERS + z) * PLANE
            pairs += [(at + i, at + (i ^ turn[core])) for i in range(PLANE)]
    return pairs


def climbs(stage):
    steps = [[(z, (z + 1) % LAYERS) for z in range(LAYERS)]]
    steps.append([(z, z + 1) for z in range(stage - 1, LAYERS - 1)])
    if stage == LAYERS - 1:
        steps[1].append((LAYERS - 1, LAYERS - 2))
    pairs = []
    for core in range(2):
        for source, target in steps[core]:
            at, to = [(core * LAYERS + z) * PLANE for z in (source, target)]
            pairs += [(at + i, to + i) for i in range(PLANE)]
    return pairs


def tied(value, after):
    return lax.optimization_barrier((value, *after))[0] if after else value


def fit_kernel(flags, own, near, far, factor, out):
    wide = own.shape[0]

    @pl.when(flags[0] == 1)
    def _():
        total = lax.dot_general(
            jnp.concatenate([own[...], near[...], far[...]]),
            factor[...],
            (((1,), (1,)), ((), ())),
            preferred_element_type=jnp.float32,
        ).astype(out.dtype)
        turned = flags[1] * wide
        places = [
            0,
            pl.multiple_of(2 * wide - turned, 32),
            pl.multiple_of(wide + turned, 32),
            3 * wide,
        ]
        for i, at in enumerate(places):
            out[pl.ds(at, wide), :] = total[i * wide : (i + 1) * wide]

    @pl.when(flags[0] == 0)
    def _():
        out[...] = jnp.zeros(out.shape, out.dtype)


def fit(flags, pieces, factor):
    depth = factor.shape[1]
    wide = sum(piece.shape[0] for piece in pieces)
    rows = factor.shape[0]
    step = min(rows, 256)
    return pl.pallas_call(
        fit_kernel,
        out_shape=jax.ShapeDtypeStruct((wide, rows), jnp.bfloat16),
        grid_spec=pltpu.PrefetchScalarGridSpec(
            num_scalar_prefetch=1,
            grid=(rows // step,),
            in_specs=[pl.BlockSpec(piece.shape, lambda i, flags: (0, 0)) for piece in pieces]
            + [pl.BlockSpec((step, depth), lambda i, flags: (i * flags[0], 0))],
            out_specs=pl.BlockSpec((wide, step), lambda i, flags: (0, i)),
        ),
        compiler_params=pltpu.CompilerParams(vmem_limit_bytes=40 << 20),
        cost_estimate=pl.CostEstimate(
            flops=2 * wide * depth * rows,
            bytes_accessed=2 * (depth * (wide + rows) + wide * rows),
            transcendentals=0,
        ),
    )(flags, *pieces, factor)


def shards_stacked(metric_factor, three_centre, occ_energy, virt_energy):
    aux_id = lax.axis_index("aux")
    pair_id = lax.axis_index("pair")
    layer = pair_id // PLANE
    place = pair_id % PLANE
    share_rows = three_centre.shape[1]
    pair_count = LAYERS * PLANE
    pairs_total = share_rows * pair_count
    share_cols = pairs_total // 2
    rows = metric_factor.shape[0]
    own = three_centre.T
    needed = jnp.logical_or(aux_id == 0, layer >= LAYERS // 2)
    crossed = []

    def cross(piece, turn, after):
        after = [*crossed[-2:][: max(len(crossed) - 1, 0)][:1], *after]
        crossed.append(lax.ppermute(tied(piece, after), AXES, along(turn)))
        return crossed[-1]

    def first(piece, after=()):
        return [piece, cross(piece, TURN, after)]

    def second(held, after=()):
        return [*held, cross(jnp.concatenate(held), TURN[::-1], after)]

    def climb(piece, stage, after=()):
        return lax.ppermute(tied(piece, after), AXES, climbs(stage))

    flags = jnp.stack([needed, aux_id == 0]).astype(jnp.int32)

    def fitted_of(pieces):
        partial = fit(flags, pieces, metric_factor)
        other = lax.ppermute(partial, "aux", [(0, 1), (1, 0)])
        total = partial.astype(jnp.float32) + other.astype(jnp.float32)
        return partial, total.astype(jnp.bfloat16)

    above_1 = climb(own, 1)
    held_0 = first(own)
    plane_0 = second(held_0)
    held_1 = first(above_1)
    above_2 = climb(above_1, 2, held_0[1:])
    plane_1 = second(held_1)
    held_2 = first(above_2)
    turning = jnp.logical_and(aux_id == 1, layer == LAYERS - 1)
    above_3 = climb(jnp.where(turning, own, above_2), 3, held_1[1:])
    plane_2 = second(held_2)
    partial_0, fitted_0 = fitted_of(plane_0)
    held_3 = first(above_3, [partial_0])
    partial_1, fitted_1 = fitted_of(plane_1)
    plane_3 = second(held_3, [partial_1])
    partial_2, fitted_2 = fitted_of(plane_2)
    plane_3[2] = tied(plane_3[2], [partial_2])
    fitted = jnp.concatenate([fitted_0, fitted_1, fitted_2, fitted_of(plane_3)[1]])
    blocks = fitted.reshape(pair_count, share_rows, rows)
    ordered = []
    for z in range(LAYERS):
        slot = (layer - z) % LAYERS
        for where in range(PLANE):
            offset = place ^ where
            at = slot * PLANE + offset
            ordered.append(lax.dynamic_index_in_dim(blocks, at, 0, keepdims=False))
    fitted = jnp.concatenate(ordered)
    own_share = lax.dynamic_slice_in_dim(fitted, aux_id * share_cols, share_cols, 0)
    partial_tiles = nt_dot(fitted, own_share).astype(jnp.bfloat16)
    tiles = lax.all_to_all(
        partial_tiles.reshape(pair_count, share_rows, share_cols), "pair", 0, 0, tiled=True
    )
    return outputs(tiles, occ_energy, virt_energy)


def solution(mesh):
    in_specs = (P("pair", "aux"), P("aux", "pair"), P(), P())
    out_specs = (P("pair", "aux"), P())
    stacked = mesh.shape["aux"] == 2 and mesh.shape["pair"] == LAYERS * PLANE
    return jax.shard_map(
        shards_stacked if stacked else shards_any,
        mesh=mesh,
        in_specs=in_specs,
        out_specs=out_specs,
        check_vma=False,
    )
```

time: 439 us -> 329 us (0.75)
  waiting for transfers between devices: 351 us -> 161 us
  starting transfers between devices: 7.03 us -> 68.4 us
  Pallas kernels: 0 us -> 47.3 us
  matrix products: 40.1 us -> 3.89 us
  other arithmetic: 5.66 us -> 19.1 us
  between operations: 15.6 us -> 3.08 us
  local copies, waits for them, and re-layouts: 0.83 us -> 7.09 us
    all_gather x2 -> x0, waiting for transfers between devices: 290 us -> none  [the longest x1 277 us: shards(): lax.all_gather(three_centre, 'pair', axis=1, tiled=True)]
    ppermute x0 -> x15, waiting for transfers between devices: none -> 113 us  [the longest x8 71.7 us: cross(): crossed.append(lax.ppermute(tied(piece, after), AXES, along(turn)))]
    ppermute x0 -> x15, starting transfers between devices: none -> 51.1 us  [the longest x3 26.8 us: climb(): return lax.ppermute(tied(piece, after), AXES, climbs(stage))]
    pallas_call x0 -> x4, Pallas kernels: none -> 47.3 us  [fit(): pl.pallas_call(fit_kernel, out_shape=jax.ShapeDtypeStruct((wide, rows), j...]
    dot_general x2 -> x1, matrix products: 40.1 us -> 3.89 us  [nt_dot(): lax.dot_general(left, right, (((1,), (1,)), ((), ())), preferred_element_...]
    concatenate x0 -> x5, other arithmetic: none -> 14 us  [the longest x4 13.6 us: second(): return [*held, cross(jnp.concatenate(held), TURN[::-1], after)]]
    reduce_scatter x1 -> x0, waiting for transfers between devices: 12.8 us -> none  [shards(): lax.psum_scatter(partial_fit, 'aux', scatter_dimension=1, tiled=True)]
    all_to_all x1, starting transfers between devices: 6.92 us -> 17.3 us  [shards_stacked(): lax.all_to_all(partial_tiles.reshape(pair_count, share_rows, share_cols),...]
  transfers between devices with their start and end apart: 4 -> 16, of which waited for: 4 -> 10; matrix products, arithmetic and copies ran while one was open for 0% -> 5% of each run, Pallas kernels for 0% -> 14%
where the time goes in v2:
time: 329 us; the launch traced here: 328 us
  waiting for transfers between devices  161 us (49%)
  starting transfers between devices  68.4 us (21%)
  Pallas kernels  47.3 us (14%)
  other arithmetic  19.1 us (6%)
  blocking collectives  18.2 us (6%)
  local copies, waits for them, and re-layouts  7.09 us (2%)
  matrix products  3.89 us (1%)
    ppermute x8, waiting for transfers between devices, cross(): crossed.append(lax.ppermute(tied(piece, after), AXES, along(turn)))  71.7 us
    all_to_all x1, waiting for transfers between devices, shards_stacked(): lax.all_to_all(partial_tiles.reshape(pair_count, share_rows, share_cols),...  47.4 us
    pallas_call x4, Pallas kernels, fit(): pl.pallas_call(fit_kernel, out_shape=jax.ShapeDtypeStruct((wide, rows), j...  47.3 us
    ppermute x3, waiting for transfers between devices, climb(): return lax.ppermute(tied(piece, after), AXES, climbs(stage))  40.3 us
    ppermute x3, starting transfers between devices, climb(): return lax.ppermute(tied(piece, after), AXES, climbs(stage))  26.8 us
    ppermute x8, starting transfers between devices, cross(): crossed.append(lax.ppermute(tied(piece, after), AXES, along(turn)))  23.6 us
    all_to_all x1, blocking collectives, total_of(): return jnp.sum(lax.all_to_all(sent, axes, 0, 0, tiled=True)[:, 0, 0])  18.2 us
    all_to_all x1, starting transfers between devices, shards_stacked(): lax.all_to_all(partial_tiles.reshape(pair_count, share_rows, share_cols),...  17.3 us
  transfers between devices with their start and end apart: 16, of which 10 were waited for; matrix products, arithmetic and copies ran while one was open for 5% of the time, Pallas kernels for 14%

profile of v2, /device:TPU:0, one launch (start us, length us, event | category | flops | bytes accessed | tf_op | source)
XLA Modules:
  0.0 327.6 jit_solution(14129123752603070397)
XLA Ops:
  0.6 4.8 %collective-permute-start = (bf16[96,8192]{1,0:T(8,128)(2,1)}, bf16[96,8192]{1,0:T(8,128)(2,1)S(1)}, u32[]{:S(2)}, u32[]{:S(2)}) collective-permute-start(bf16[96,8192]{1,0:T(8,128)(2,1)} %bitcast.39), channel_id=1, source_target_pairs={{0,1},{1,0},{2,3},{3,2},{4,5},{5,4},{6,7},{7,6},{8,9},{9,8},{10,11... | collective-permute-start | bytes 4718600 | tf_op jit(solution)/shard_map/ppermute | solution.py:160
  5.5 3.5 %collective-permute-start.3 = (bf16[96,8192]{1,0:T(8,128)(2,1)}, bf16[96,8192]{1,0:T(8,128)(2,1)}, u32[]{:S(2)}, u32[]{:S(2)}) collective-permute-start(bf16[96,8192]{1,0:T(8,128)(2,1)} %bitcast.40), channel_id=1, source_target_pairs={{0,4},{1,5},{2,6},{3,7},{4,8},{5,9},{6,10},{7,11},{8,12},{9,13},{1... | collective-permute-start | bytes 4718600 | tf_op jit(solution)/shard_map/ppermute | solution.py:170
  9.0 15.1 %collective-permute-done.near = bf16[96,8192]{1,0:T(8,128)(2,1)S(1)} collective-permute-done((bf16[96,8192]{1,0:T(8,128)(2,1)}, bf16[96,8192]{1,0:T(8,128)(2,1)S(1)}, u32[]{:S(2)}, u32[]{:S(2)}) %collective-permute-start) | collective-permute-done | bytes 1572896 | tf_op jit(solution)/shard_map/ppermute | solution.py:160
  24.1 4.1 %pad_maximum_fusion = bf16[192,8192]{1,0:T(8,128)(2,1)} fusion(bf16[96,8192]{1,0:T(8,128)(2,1)S(1)} %collective-permute-done.near, bf16[96,8192]{1,0:T(8,128)(2,1)} %bitcast.41), kind=kLoop, calls=%fused_computation.2 | loop fusion | flops 6291456 | bytes 6291456 | tf_op jit(solution)/shard_map/concatenate | solution.py:167
  28.2 3.9 %collective-permute-start.1 = (bf16[192,8192]{1,0:T(8,128)(2,1)}, bf16[192,8192]{1,0:T(8,128)(2,1)}, u32[]{:S(2)}, u32[]{:S(2)}) collective-permute-start(bf16[192,8192]{1,0:T(8,128)(2,1)} %pad_maximum_fusion), channel_id=1, source_target_pairs={{0,2},{1,3},{2,0},{3,1},{4,6},{5,7},{6,4},{7,5},{8,10},{9,11},{10,... | collective-permute-start | bytes 9437192 | tf_op jit(solution)/shard_map/ppermute | solution.py:160
  32.2 8.1 %collective-permute-done.3.own = bf16[96,8192]{1,0:T(8,128)(2,1)} collective-permute-done((bf16[96,8192]{1,0:T(8,128)(2,1)}, bf16[96,8192]{1,0:T(8,128)(2,1)}, u32[]{:S(2)}, u32[]{:S(2)}) %collective-permute-start.3) | collective-permute-done | bytes 1572896 | tf_op jit(solution)/shard_map/ppermute | solution.py:170
  40.3 3.4 %collective-permute-start.4 = (bf16[96,8192]{1,0:T(8,128)(2,1)}, bf16[96,8192]{1,0:T(8,128)(2,1)}, u32[]{:S(2)}, u32[]{:S(2)}) collective-permute-start(bf16[96,8192]{1,0:T(8,128)(2,1)} %collective-permute-done.3.own), channel_id=1, source_target_pairs={{0,1},{1,0},{2,3},{3,2},{4,5},{5,4},{6,7},{7,6},{8,9},{9,8},{10,11... | collective-permute-start | bytes 4718600 | tf_op jit(solution)/shard_map/ppermute | solution.py:160
  43.7 5.9 %collective-permute-start.7 = (bf16[96,8192]{1,0:T(8,128)(2,1)}, bf16[96,8192]{1,0:T(8,128)(2,1)S(1)}, u32[]{:S(2)}, u32[]{:S(2)}) collective-permute-start(bf16[96,8192]{1,0:T(8,128)(2,1)} %collective-permute-done.3.own), channel_id=1, source_target_pairs={{0,4},{1,5},{2,6},{3,7},{4,8},{5,9},{6,10},{7,11},{8,12},{9,13},{1... | collective-permute-start | bytes 4718600 | tf_op jit(solution)/shard_map/ppermute | solution.py:170
  49.6 13.3 %collective-permute-done.4.near = bf16[96,8192]{1,0:T(8,128)(2,1)} collective-permute-done((bf16[96,8192]{1,0:T(8,128)(2,1)}, bf16[96,8192]{1,0:T(8,128)(2,1)}, u32[]{:S(2)}, u32[]{:S(2)}) %collective-permute-start.4) | collective-permute-done | bytes 1572896 | tf_op jit(solution)/shard_map/ppermute | solution.py:160
  62.9 8.2 %collective-permute-done.7.own = bf16[96,8192]{1,0:T(8,128)(2,1)S(1)} collective-permute-done((bf16[96,8192]{1,0:T(8,128)(2,1)}, bf16[96,8192]{1,0:T(8,128)(2,1)S(1)}, u32[]{:S(2)}, u32[]{:S(2)}) %collective-permute-start.7) | collective-permute-done | bytes 1572896 | tf_op jit(solution)/shard_map/ppermute | solution.py:170
  71.1 2.4 collective-permute-start.8
  73.5 3.9 %pad_maximum_fusion.1 = bf16[192,8192]{1,0:T(8,128)(2,1)} fusion(bf16[96,8192]{1,0:T(8,128)(2,1)} %collective-permute-done.4.near, bf16[96,8192]{1,0:T(8,128)(2,1)} %collective-permute-done.3.own), kind=kLoop, calls=%fused_computation.3 | loop fusion | flops 6291456 | bytes 6291456 | tf_op jit(solution)/shard_map/concatenate | solution.py:167
  77.4 2.4 collective-permute-start.5
  81.2 17.4 %collective-permute-start.11 = (bf16[96,8192]{1,0:T(8,128)(2,1)}, bf16[96,8192]{1,0:T(8,128)(2,1)}, u32[]{:S(2)}, u32[]{:S(2)}) collective-permute-start(bf16[96,8192]{1,0:T(8,128)(2,1)} %broadcast_select_fusion), channel_id=1, source_target_pairs={{0,4},{1,5},{2,6},{3,7},{4,8},{5,9},{6,10},{7,11},{8,12},{9,13},{1... | collective-permute-start | bytes 4718600 | tf_op jit(solution)/shard_map/ppermute | solution.py:170
  100.1 11.6 %shard_map.59 = bf16[384,1024]{1,0:T(8,128)(2,1)S(1)} custom-call(s32[2]{0:T(128)S(1)} %add_convert_fusion.4.flags, bf16[96,8192]{1,0:T(8,128)(2,1)S(1)} %bitcast.42, bf16[96,8192]{1,0:T(8,128)(2,1)S(1)} %copy-done.2, bf16[192,8192]{1,0:T(8,128)(2,1)} %collective-permute-done.1.far, bf16[1024,8192]{1,0:T(8,128)(2,1)} %factor.7), custom_call_target="tpu_custom_call" | custom-call | flops 6442450944 | bytes 23855104 | tf_op jit(solution)/shard_map/pallas_call | solution.py:125
  111.7 24.0 %collective-permute-done.11.own = bf16[96,8192]{1,0:T(8,128)(2,1)} collective-permute-done((bf16[96,8192]{1,0:T(8,128)(2,1)}, bf16[96,8192]{1,0:T(8,128)(2,1)}, u32[]{:S(2)}, u32[]{:S(2)}) %collective-permute-start.11) | collective-permute-done | bytes 1572896 | tf_op jit(solution)/shard_map/ppermute | solution.py:170
  135.7 2.2 collective-permute-start.12
  137.9 1.9 pad_maximum_fusion.2
  139.8 2.2 collective-permute-start.9
  142.0 16.2 %collective-permute-done.12.near = bf16[96,8192]{1,0:T(8,128)(2,1)S(1)} collective-permute-done((bf16[96,8192]{1,0:T(8,128)(2,1)}, bf16[96,8192]{1,0:T(8,128)(2,1)S(1)}, u32[]{:S(2)}, u32[]{:S(2)}) %collective-permute-start.12) | collective-permute-done | bytes 1572896 | tf_op jit(solution)/shard_map/ppermute | solution.py:160
  158.2 3.7 %pad_maximum_fusion.3 = bf16[192,8192]{1,0:T(8,128)(2,1)} fusion(bf16[96,8192]{1,0:T(8,128)(2,1)S(1)} %collective-permute-done.12.near, bf16[96,8192]{1,0:T(8,128)(2,1)} %collective-permute-done.11.own), kind=kLoop, calls=%fused_computation.5 | loop fusion | flops 6291456 | bytes 6291456 | tf_op jit(solution)/shard_map/concatenate | solution.py:167
  161.9 12.5 %shard_map.60 = bf16[384,1024]{1,0:T(8,128)(2,1)S(1)} custom-call(s32[2]{0:T(128)S(1)} %add_convert_fusion.4.flags, bf16[96,8192]{1,0:T(8,128)(2,1)} %collective-permute-done.3.own, bf16[96,8192]{1,0:T(8,128)(2,1)} %collective-permute-done.4.near, bf16[192,8192]{1,0:T(8,128)(2,1)} %collective-permute-done.5.far, bf16[1024,8192]{1,0:T(8,128)(2,1)} %factor.7), custom_call_target="tpu_custom_call" | custom-call | flops 6442450944 | bytes 23855104 | tf_op jit(solution)/shard_map/pallas_call | solution.py:125
  175.3 3.7 %collective-permute-done.9.far = bf16[192,8192]{1,0:T(8,128)(2,1)S(1)} collective-permute-done((bf16[192,8192]{1,0:T(8,128)(2,1)S(1)}, bf16[192,8192]{1,0:T(8,128)(2,1)S(1)}, u32[]{:S(2)}, u32[]{:S(2)}) %collective-permute-start.9) | collective-permute-done | bytes 3145760 | tf_op jit(solution)/shard_map/ppermute | solution.py:160
  180.7 2.2 collective-permute-start.13
  183.6 1.9 copy-done.8
  185.5 11.1 %shard_map.61 = bf16[384,1024]{1,0:T(8,128)(2,1)S(1)} custom-call(s32[2]{0:T(128)S(1)} %add_convert_fusion.4.flags, bf16[96,8192]{1,0:T(8,128)(2,1)S(1)} %collective-permute-done.7.own, bf16[96,8192]{1,0:T(8,128)(2,1)} %collective-permute-done.8.near, bf16[192,8192]{1,0:T(8,128)(2,1)S(1)} %copy-done.8, bf16[1024,8192]{1,0:T(8,128)(2,1)} %factor.7), custom_call_target="tpu_custom_call" | custom-call | flops 6442450944 | bytes 23855104 | tf_op jit(solution)/shard_map/pallas_call | solution.py:125
  196.8 23.4 %collective-permute-done.13.far = bf16[192,8192]{1,0:T(8,128)(2,1)} collective-permute-done((bf16[192,8192]{1,0:T(8,128)(2,1)}, bf16[192,8192]{1,0:T(8,128)(2,1)}, u32[]{:S(2)}, u32[]{:S(2)}) %collective-permute-start.13) | collective-permute-done | bytes 3145760 | tf_op jit(solution)/shard_map/ppermute | solution.py:160
  220.2 12.0 %shard_map.62 = bf16[384,1024]{1,0:T(8,128)(2,1)S(1)} custom-call(s32[2]{0:T(128)S(1)} %add_convert_fusion.4.flags, bf16[96,8192]{1,0:T(8,128)(2,1)} %collective-permute-done.11.own, bf16[96,8192]{1,0:T(8,128)(2,1)S(1)} %collective-permute-done.12.near, bf16[192,8192]{1,0:T(8,128)(2,1)} %collective-permute-done.13.far, bf16[1024,8192]{1,0:T(8,128)(2,1)} %factor.7), custom_call_target="tpu_custom_call" | custom-call | flops 6442450944 | bytes 23855104 | tf_op jit(solution)/shard_map/pallas_call | solution.py:125
  235.8 3.9 %convolution_convert_fusion = bf16[1536,768]{1,0:T(8,128)(2,1)} fusion(bf16[1536,1024]{1,0:T(8,128)(2,1)S(1)} %bitcast_dynamic-update-slice_fusion, s32[]{:T(128)S(6)} %select_n.115), kind=kOutput, calls=%fused_computation.1 | convolution fusion | flops 2417098752 | bytes 7077892 | tf_op jit(solution)/shard_map/dot_general | solution.py:23
  239.6 17.3 %all-to-all-start = ((bf16[16,96,768]{2,1,0:T(8,128)(2,1)}), bf16[16,96,768]{2,1,0:T(8,128)(2,1)S(1)}, u32[]{:S(2)}, u32[]{:S(2)}) async-start(bf16[16,96,768]{2,1,0:T(8,128)(2,1)} %bitcast.59), calls=%async_computation | async-start | bytes 4718592 | tf_op jit(solution)/shard_map/all_to_all | solution.py:208
  257.2 47.4 %all-to-all-done = bf16[16,96,768]{2,1,0:T(8,128)(2,1)S(1)} async-done(((bf16[16,96,768]{2,1,0:T(8,128)(2,1)}), bf16[16,96,768]{2,1,0:T(8,128)(2,1)S(1)}, u32[]{:S(2)}, u32[]{:S(2)}) %all-to-all-start) | async-done | bytes 2359328 | tf_op jit(solution)/shard_map/all_to_all | solution.py:208
  307.0 18.2 %all_to_all.10 = f32[32,8,128]{2,1,0:T(8,128)S(1)} all-to-all(f32[32,8,128]{2,1,0:T(8,128)S(1)} %broadcast_in_dim.2), channel_id=1, replica_groups=mesh['aux'=2,'pair'=16] {'aux','pair'}, dimensions={0} | all-to-all | bytes 262144 | tf_op jit(solution)/shard_map/all_to_all | solution.py:19
  (63 shorter events, 12.7 us)
Async XLA Ops:
  0.6 23.4 %collective-permute-start = (bf16[96,8192]{1,0:T(8,128)(2,1)}, bf16[96,8192]{1,0:T(8,128)(2,1)S(1)}, u32[]{:S(2)}, u32[]{:S(2)}) collective-permute-start(bf16[96,8192]{1,0:T(8,128)(2,1)} %bitcast.39), channel_id=1, source_target_pairs={{0,1},{1,0},{2,3},{3,2},{4,5},{5,4},{6,7},{7,6},{8,9},{9,8},{10,11... | collective-permute-start | bytes 4718600 | tf_op jit(solution)/shard_map/ppermute | solution.py:160
  5.5 34.8 %collective-permute-start.3 = (bf16[96,8192]{1,0:T(8,128)(2,1)}, bf16[96,8192]{1,0:T(8,128)(2,1)}, u32[]{:S(2)}, u32[]{:S(2)}) collective-permute-start(bf16[96,8192]{1,0:T(8,128)(2,1)} %bitcast.40), channel_id=1, source_target_pairs={{0,4},{1,5},{2,6},{3,7},{4,8},{5,9},{6,10},{7,11},{8,12},{9,13},{1... | collective-permute-start | bytes 4718600 | tf_op jit(solution)/shard_map/ppermute | solution.py:170
  24.1 4.1 %copy-start.1 = (bf16[96,8192]{1,0:T(8,128)(2,1)}, bf16[96,8192]{1,0:T(8,128)(2,1)S(1)}, u32[]{:S(2)}) copy-start(bf16[96,8192]{1,0:T(8,128)(2,1)S(1)} %collective-permute-done.near) | copy-start | bytes 4718596
  28.2 49.2 %collective-permute-start.1 = (bf16[192,8192]{1,0:T(8,128)(2,1)}, bf16[192,8192]{1,0:T(8,128)(2,1)}, u32[]{:S(2)}, u32[]{:S(2)}) collective-permute-start(bf16[192,8192]{1,0:T(8,128)(2,1)} %pad_maximum_fusion), channel_id=1, source_target_pairs={{0,2},{1,3},{2,0},{3,1},{4,6},{5,7},{6,4},{7,5},{8,10},{9,11},{10,... | collective-permute-start | bytes 9437192 | tf_op jit(solution)/shard_map/ppermute | solution.py:160
  40.3 22.6 %collective-permute-start.4 = (bf16[96,8192]{1,0:T(8,128)(2,1)}, bf16[96,8192]{1,0:T(8,128)(2,1)}, u32[]{:S(2)}, u32[]{:S(2)}) collective-permute-start(bf16[96,8192]{1,0:T(8,128)(2,1)} %collective-permute-done.3.own), channel_id=1, source_target_pairs={{0,1},{1,0},{2,3},{3,2},{4,5},{5,4},{6,7},{7,6},{8,9},{9,8},{10,11... | collective-permute-start | bytes 4718600 | tf_op jit(solution)/shard_map/ppermute | solution.py:160
  43.7 27.4 %collective-permute-start.7 = (bf16[96,8192]{1,0:T(8,128)(2,1)}, bf16[96,8192]{1,0:T(8,128)(2,1)S(1)}, u32[]{:S(2)}, u32[]{:S(2)}) collective-permute-start(bf16[96,8192]{1,0:T(8,128)(2,1)} %collective-permute-done.3.own), channel_id=1, source_target_pairs={{0,4},{1,5},{2,6},{3,7},{4,8},{5,9},{6,10},{7,11},{8,12},{9,13},{1... | collective-permute-start | bytes 4718600 | tf_op jit(solution)/shard_map/ppermute | solution.py:170
  49.6 30.2 %copy-start = (bf16[8192,96]{0,1:T(8,128)(2,1)S(1)}, bf16[8192,96]{0,1:T(8,128)(2,1)}, u32[]{:S(2)}) copy-start(bf16[8192,96]{0,1:T(8,128)(2,1)} %param.5) | copy-start | bytes 4718596
  71.1 40.6 %collective-permute-start.8 = (bf16[96,8192]{1,0:T(8,128)(2,1)S(1)}, bf16[96,8192]{1,0:T(8,128)(2,1)}, u32[]{:S(2)}, u32[]{:S(2)}) collective-permute-start(bf16[96,8192]{1,0:T(8,128)(2,1)S(1)} %collective-permute-done.7.own), channel_id=1, source_target_pairs={{0,1},{1,0},{2,3},{3,2},{4,5},{5,4},{6,7},{7,6},{8,9},{9,8},{10,11... | collective-permute-start | bytes 4718600 | tf_op jit(solution)/shard_map/ppermute | solution.py:160
  77.4 62.4 %collective-permute-start.5 = (bf16[192,8192]{1,0:T(8,128)(2,1)}, bf16[192,8192]{1,0:T(8,128)(2,1)}, u32[]{:S(2)}, u32[]{:S(2)}) collective-permute-start(bf16[192,8192]{1,0:T(8,128)(2,1)} %pad_maximum_fusion.1), channel_id=1, source_target_pairs={{0,2},{1,3},{2,0},{3,1},{4,6},{5,7},{6,4},{7,5},{8,10},{9,11},{10,... | collective-permute-start | bytes 9437192 | tf_op jit(solution)/shard_map/ppermute | solution.py:160
  81.2 54.5 %collective-permute-start.11 = (bf16[96,8192]{1,0:T(8,128)(2,1)}, bf16[96,8192]{1,0:T(8,128)(2,1)}, u32[]{:S(2)}, u32[]{:S(2)}) collective-permute-start(bf16[96,8192]{1,0:T(8,128)(2,1)} %broadcast_select_fusion), channel_id=1, source_target_pairs={{0,4},{1,5},{2,6},{3,7},{4,8},{5,9},{6,10},{7,11},{8,12},{9,13},{1... | collective-permute-start | bytes 4718600 | tf_op jit(solution)/shard_map/ppermute | solution.py:170
  98.7 1.4 copy-start.2
  111.7 46.5 %copy-start.3 = (bf16[384,1024]{1,0:T(8,128)(2,1)}, bf16[384,1024]{1,0:T(8,128)(2,1)S(1)}, u32[]{:S(2)}) copy-start(bf16[384,1024]{1,0:T(8,128)(2,1)S(1)} %shard_map.59) | copy-start | bytes 2359300
  135.7 22.5 %collective-permute-start.12 = (bf16[96,8192]{1,0:T(8,128)(2,1)}, bf16[96,8192]{1,0:T(8,128)(2,1)S(1)}, u32[]{:S(2)}, u32[]{:S(2)}) collective-permute-start(bf16[96,8192]{1,0:T(8,128)(2,1)} %collective-permute-done.11.own), channel_id=1, source_target_pairs={{0,1},{1,0},{2,3},{3,2},{4,5},{5,4},{6,7},{7,6},{8,9},{9,8},{10,11... | collective-permute-start | bytes 4718600 | tf_op jit(solution)/shard_map/ppermute | solution.py:160
  139.8 39.2 %collective-permute-start.9 = (bf16[192,8192]{1,0:T(8,128)(2,1)S(1)}, bf16[192,8192]{1,0:T(8,128)(2,1)S(1)}, u32[]{:S(2)}, u32[]{:S(2)}) collective-permute-start(bf16[192,8192]{1,0:T(8,128)(2,1)S(1)} %pad_maximum_fusion.2), channel_id=1, source_target_pairs={{0,2},{1,3},{2,0},{3,1},{4,6},{5,7},{6,4},{7,5},{8,10},{9,11},{10,... | collective-permute-start | bytes 9437192 | tf_op jit(solution)/shard_map/ppermute | solution.py:160
  174.4 0.9 copy-start.5
  179.0 1.7 copy-start.7
  180.7 39.5 %collective-permute-start.13 = (bf16[192,8192]{1,0:T(8,128)(2,1)}, bf16[192,8192]{1,0:T(8,128)(2,1)}, u32[]{:S(2)}, u32[]{:S(2)}) collective-permute-start(bf16[192,8192]{1,0:T(8,128)(2,1)} %pad_maximum_fusion.3), channel_id=1, source_target_pairs={{0,2},{1,3},{2,0},{3,1},{4,6},{5,7},{6,4},{7,5},{8,10},{9,11},{10,... | collective-permute-start | bytes 9437192 | tf_op jit(solution)/shard_map/ppermute | solution.py:160
  183.1 49.2 %collective-permute-start.2 = (bf16[384,1024]{1,0:T(8,128)(2,1)}, bf16[384,1024]{1,0:T(8,128)(2,1)S(1)}, u32[]{:S(2)}, u32[]{:S(2)}) collective-permute-start(bf16[384,1024]{1,0:T(8,128)(2,1)} %copy-done.3), channel_id=1, source_target_pairs={{0,16},{16,0},{1,17},{17,1},{2,18},{18,2},{3,19},{19,3},{4,20},{20... | collective-permute-start | bytes 2359304 | tf_op jit(solution)/shard_map/ppermute | solution.py:176
  183.1 49.5 %collective-permute-start.6 = (bf16[384,1024]{1,0:T(8,128)(2,1)}, bf16[384,1024]{1,0:T(8,128)(2,1)S(1)}, u32[]{:S(2)}, u32[]{:S(2)}) collective-permute-start(bf16[384,1024]{1,0:T(8,128)(2,1)} %copy-done.5), channel_id=1, source_target_pairs={{0,16},{16,0},{1,17},{17,1},{2,18},{18,2},{3,19},{19,3},{4,20},{20... | collective-permute-start | bytes 2359304 | tf_op jit(solution)/shard_map/ppermute | solution.py:176
  183.6 1.9 copy-start.8
  196.7 35.6 %copy-start.4 = (bf16[384,1024]{1,0:T(8,128)(2,1)S(1)}, bf16[384,1024]{1,0:T(8,128)(2,1)}, u32[]{:S(2)}) copy-start(bf16[384,1024]{1,0:T(8,128)(2,1)} %copy-done.3) | copy-start | bytes 2359300
  196.7 36.0 %copy-start.6 = (bf16[384,1024]{1,0:T(8,128)(2,1)S(1)}, bf16[384,1024]{1,0:T(8,128)(2,1)}, u32[]{:S(2)}) copy-start(bf16[384,1024]{1,0:T(8,128)(2,1)} %copy-done.5) | copy-start | bytes 2359300
  196.7 36.3 %collective-permute-start.10 = (bf16[384,1024]{1,0:T(8,128)(2,1)S(1)}, bf16[384,1024]{1,0:T(8,128)(2,1)S(1)}, u32[]{:S(2)}, u32[]{:S(2)}) collective-permute-start(bf16[384,1024]{1,0:T(8,128)(2,1)S(1)} %shard_map.61), channel_id=1, source_target_pairs={{0,16},{16,0},{1,17},{17,1},{2,18},{18,2},{3,19},{19,3},{4,20},{20... | collective-permute-start | bytes 2359304 | tf_op jit(solution)/shard_map/ppermute | solution.py:176
  232.2 2.4 collective-permute-start.14
  239.6 17.3 %copy-start.9 = (f32[768]{0:T(1024)S(1)}, f32[768]{0:T(1024)}, u32[]{:S(2)}) copy-start(f32[768]{0:T(1024)} %param.7) | copy-start | bytes 9220
  239.6 17.3 %copy-start.10 = (f32[2]{0:T(128)S(1)}, f32[2]{0:T(128)}, u32[]{:S(2)}) copy-start(f32[2]{0:T(128)} %param.6) | copy-start | bytes 28
  239.6 64.9 %all-to-all-start = ((bf16[16,96,768]{2,1,0:T(8,128)(2,1)}), bf16[16,96,768]{2,1,0:T(8,128)(2,1)S(1)}, u32[]{:S(2)}, u32[]{:S(2)}) async-start(bf16[16,96,768]{2,1,0:T(8,128)(2,1)} %bitcast.59), calls=%async_computation | async-start | bytes 4718592 | tf_op jit(solution)/shard_map/all_to_all | solution.py:208

commit v3 on v2

--- a/solution.py
+++ b/solution.py
@@ -91,13 +91,13 @@
     return lax.optimization_barrier((value, *after))[0] if after else value
 
 
-def fit_kernel(flags, own, near, far, factor, out):
+def fit_kernel(flags, own, near, far, both, factor, out):
     wide = own.shape[0]
 
     @pl.when(flags[0] == 1)
     def _():
         total = lax.dot_general(
-            jnp.concatenate([own[...], near[...], far[...]]),
+            jnp.concatenate([own[...], near[...], far[...], both[...]]),
             factor[...],
             (((1,), (1,)), ((), ())),
             preferred_element_type=jnp.float32,
@@ -155,16 +155,15 @@
     needed = jnp.logical_or(aux_id == 0, layer >= LAYERS // 2)
     crossed = []
 
-    def cross(piece, turn, after):
-        after = [*crossed[-2:][: max(len(crossed) - 1, 0)][:1], *after]
+    def cross(piece, turn, after=()):
+        after = [*crossed[-4:][: max(len(crossed) - 3, 0)][:1], *after]
         crossed.append(lax.ppermute(tied(piece, after), AXES, along(turn)))
         return crossed[-1]
 
-    def first(piece, after=()):
-        return [piece, cross(piece, TURN, after)]
-
-    def second(held, after=()):
-        return [*held, cross(jnp.concatenate(held), TURN[::-1], after)]
+    def spread(piece, after=(), near=None):
+        near = cross(piece, TURN) if near is None else near
+        far = cross(piece, TURN[::-1])
+        return [piece, near, far, cross(near, TURN[::-1], after)]
 
     def climb(piece, stage, after=()):
         return lax.ppermute(tied(piece, after), AXES, climbs(stage))
@@ -178,21 +177,18 @@
         return partial, total.astype(jnp.bfloat16)
 
     above_1 = climb(own, 1)
-    held_0 = first(own)
-    plane_0 = second(held_0)
-    held_1 = first(above_1)
-    above_2 = climb(above_1, 2, held_0[1:])
-    plane_1 = second(held_1)
-    held_2 = first(above_2)
+    plane_0 = spread(own)
+    above_2 = climb(above_1, 2, plane_0[1:2])
+    plane_1 = spread(above_1)
     turning = jnp.logical_and(aux_id == 1, layer == LAYERS - 1)
-    above_3 = climb(jnp.where(turning, own, above_2), 3, held_1[1:])
-    plane_2 = second(held_2)
+    above_3 = climb(jnp.where(turning, own, above_2), 3, plane_1[1:2])
     partial_0, fitted_0 = fitted_of(plane_0)
-    held_3 = first(above_3, [partial_0])
+    plane_2 = spread(above_2)
     partial_1, fitted_1 = fitted_of(plane_1)
-    plane_3 = second(held_3, [partial_1])
+    near_3 = climb(jnp.where(turning, plane_0[1], plane_2[1]), 3)
+    plane_3 = spread(above_3, [], near_3)
     partial_2, fitted_2 = fitted_of(plane_2)
-    plane_3[2] = tied(plane_3[2], [partial_2])
+    plane_3[3] = tied(plane_3[3], [partial_2])
     fitted = jnp.concatenate([fitted_0, fitted_1, fitted_2, fitted_of(plane_3)[1]])
     blocks = fitted.reshape(pair_count, share_rows, rows)
     ordered = []

time: 329 us -> 298 us (0.906)
  waiting for transfers between devices: 161 us -> 134 us
  other arithmetic: 19.1 us -> 9.62 us
  starting transfers between devices: 68.4 us -> 76.6 us
  local copies, waits for them, and re-layouts: 7.09 us -> 3.74 us
    ppermute x8 -> x11, waiting for transfers between devices: 71.7 us -> 13 us  [cross(): crossed.append(lax.ppermute(tied(piece, after), AXES, along(turn)))]
    ppermute x3 -> x4, waiting for transfers between devices: 40.3 us -> 72.6 us  [climb(): return lax.ppermute(tied(piece, after), AXES, climbs(stage))]
    concatenate x4 -> x0, other arithmetic: 13.6 us -> none  [second(): return [*held, cross(jnp.concatenate(held), TURN[::-1], after)]]
    all_to_all x1, starting transfers between devices: 17.3 us -> 4.6 us  [shards_stacked(): lax.all_to_all(partial_tiles.reshape(pair_count, share_rows, share_cols),...]
    ppermute x3 -> x4, starting transfers between devices: 26.8 us -> 38.2 us  [climb(): return lax.ppermute(tied(piece, after), AXES, climbs(stage))]
    ppermute x8 -> x11, starting transfers between devices: 23.6 us -> 33.6 us  [cross(): crossed.append(lax.ppermute(tied(piece, after), AXES, along(turn)))]
    select_n x1 -> x2, other arithmetic: 1.34 us -> 5.47 us  [the longest x1 2.75 us: shards_stacked(): above_3 = climb(jnp.where(turning, own, above_2), 3, plane_1[1:2])]
    unnamed x37 -> x29, local copies, waits for them, and re-layouts: 6.25 us -> 2.9 us
  transfers between devices with their start and end apart: 16 -> 20, of which waited for: 10 -> 9; matrix products, arithmetic and copies ran while one was open for 5% -> 2% of each run, Pallas kernels for 14% -> 16%
where the time goes in v3:
time: 298 us; the launch traced here: 297 us
  waiting for transfers between devices  134 us (45%)
  starting transfers between devices  76.6 us (26%)
  Pallas kernels  47.3 us (16%)
  blocking collectives  18.7 us (6%)
  other arithmetic  9.62 us (3%)
  matrix products  3.9 us (1%)
  local copies, waits for them, and re-layouts  3.74 us (1%)
  between operations  3.14 us (1%)
    ppermute x4, waiting for transfers between devices, climb(): return lax.ppermute(tied(piece, after), AXES, climbs(stage))  72.6 us
    all_to_all x1, waiting for transfers between devices, shards_stacked(): lax.all_to_all(partial_tiles.reshape(pair_count, share_rows, share_cols),...  47.4 us
    pallas_call x4, Pallas kernels, fit(): pl.pallas_call(fit_kernel, out_shape=jax.ShapeDtypeStruct((wide, rows), j...  47.3 us
    ppermute x4, starting transfers between devices, climb(): return lax.ppermute(tied(piece, after), AXES, climbs(stage))  38.2 us
    ppermute x11, starting transfers between devices, cross(): crossed.append(lax.ppermute(tied(piece, after), AXES, along(turn)))  33.6 us
    all_to_all x1, blocking collectives, total_of(): return jnp.sum(lax.all_to_all(sent, axes, 0, 0, tiled=True)[:, 0, 0])  18.7 us
    ppermute x11, waiting for transfers between devices, cross(): crossed.append(lax.ppermute(tied(piece, after), AXES, along(turn)))  13 us
  transfers between devices with their start and end apart: 20, of which 9 were waited for; matrix products, arithmetic and copies ran while one was open for 2% of the time, Pallas kernels for 16%

profile of v3, /device:TPU:0, one launch (start us, length us, event | category | flops | bytes accessed | tf_op | source)
XLA Modules:
  0.0 297.3 jit_solution(7257909758806969314)
XLA Ops:
  0.6 4.9 %collective-permute-start.4 = (bf16[96,8192]{1,0:T(8,128)(2,1)}, bf16[96,8192]{1,0:T(8,128)(2,1)}, u32[]{:S(2)}, u32[]{:S(2)}) collective-permute-start(bf16[96,8192]{1,0:T(8,128)(2,1)} %bitcast.39), channel_id=1, source_target_pairs={{0,4},{1,5},{2,6},{3,7},{4,8},{5,9},{6,10},{7,11},{8,12},{9,13},{1... | collective-permute-start | bytes 4718600 | tf_op jit(solution)/shard_map/ppermute | solution.py:169
  5.6 3.4 %collective-permute-start = (bf16[96,8192]{1,0:T(8,128)(2,1)}, bf16[96,8192]{1,0:T(8,128)(2,1)S(1)}, u32[]{:S(2)}, u32[]{:S(2)}) collective-permute-start(bf16[96,8192]{1,0:T(8,128)(2,1)} %bitcast.40), channel_id=1, source_target_pairs={{0,1},{1,0},{2,3},{3,2},{4,5},{5,4},{6,7},{7,6},{8,9},{9,8},{10,11... | collective-permute-start | bytes 4718600 | tf_op jit(solution)/shard_map/ppermute | solution.py:160
  9.0 3.4 %collective-permute-start.1 = (bf16[96,8192]{1,0:T(8,128)(2,1)}, bf16[96,8192]{1,0:T(8,128)(2,1)}, u32[]{:S(2)}, u32[]{:S(2)}) collective-permute-start(bf16[96,8192]{1,0:T(8,128)(2,1)} %bitcast.41), channel_id=1, source_target_pairs={{0,2},{1,3},{2,0},{3,1},{4,6},{5,7},{6,4},{7,5},{8,10},{9,11},{10,... | collective-permute-start | bytes 4718600 | tf_op jit(solution)/shard_map/ppermute | solution.py:160
  12.4 27.1 %collective-permute-done.4.own = bf16[96,8192]{1,0:T(8,128)(2,1)} collective-permute-done((bf16[96,8192]{1,0:T(8,128)(2,1)}, bf16[96,8192]{1,0:T(8,128)(2,1)}, u32[]{:S(2)}, u32[]{:S(2)}) %collective-permute-start.4) | collective-permute-done | bytes 1572896 | tf_op jit(solution)/shard_map/ppermute | solution.py:169
  39.5 3.4 %collective-permute-start.5 = (bf16[96,8192]{1,0:T(8,128)(2,1)}, bf16[96,8192]{1,0:T(8,128)(2,1)}, u32[]{:S(2)}, u32[]{:S(2)}) collective-permute-start(bf16[96,8192]{1,0:T(8,128)(2,1)} %collective-permute-done.4.own), channel_id=1, source_target_pairs={{0,1},{1,0},{2,3},{3,2},{4,5},{5,4},{6,7},{7,6},{8,9},{9,8},{10,11... | collective-permute-start | bytes 4718600 | tf_op jit(solution)/shard_map/ppermute | solution.py:160
  42.9 4.4 %collective-permute-start.9 = (bf16[96,8192]{1,0:T(8,128)(2,1)}, bf16[96,8192]{1,0:T(8,128)(2,1)S(1)}, u32[]{:S(2)}, u32[]{:S(2)}) collective-permute-start(bf16[96,8192]{1,0:T(8,128)(2,1)} %collective-permute-done.4.own), channel_id=1, source_target_pairs={{0,4},{1,5},{2,6},{3,7},{4,8},{5,9},{6,10},{7,11},{8,12},{9,13},{1... | collective-permute-start | bytes 4718600 | tf_op jit(solution)/shard_map/ppermute | solution.py:169
  47.3 3.4 %collective-permute-start.2 = (bf16[96,8192]{1,0:T(8,128)(2,1)S(1)}, bf16[96,8192]{1,0:T(8,128)(2,1)}, u32[]{:S(2)}, u32[]{:S(2)}) collective-permute-start(bf16[96,8192]{1,0:T(8,128)(2,1)S(1)} %collective-permute-done.near), channel_id=1, source_target_pairs={{0,2},{1,3},{2,0},{3,1},{4,6},{5,7},{6,4},{7,5},{8,10},{9,11},{10,... | collective-permute-start | bytes 4718600 | tf_op jit(solution)/shard_map/ppermute | solution.py:160
  50.8 2.4 collective-permute-start.6
  53.2 8.9 %collective-permute-done.5.near = bf16[96,8192]{1,0:T(8,128)(2,1)} collective-permute-done((bf16[96,8192]{1,0:T(8,128)(2,1)}, bf16[96,8192]{1,0:T(8,128)(2,1)}, u32[]{:S(2)}, u32[]{:S(2)}) %collective-permute-start.5) | collective-permute-done | bytes 1572896 | tf_op jit(solution)/shard_map/ppermute | solution.py:160
  62.1 3.4 %collective-permute-start.7 = (bf16[96,8192]{1,0:T(8,128)(2,1)}, bf16[96,8192]{1,0:T(8,128)(2,1)}, u32[]{:S(2)}, u32[]{:S(2)}) collective-permute-start(bf16[96,8192]{1,0:T(8,128)(2,1)} %collective-permute-done.5.near), channel_id=1, source_target_pairs={{0,2},{1,3},{2,0},{3,1},{4,6},{5,7},{6,4},{7,5},{8,10},{9,11},{10,... | collective-permute-start | bytes 4718600 | tf_op jit(solution)/shard_map/ppermute | solution.py:160
  65.6 2.4 collective-permute-done.9.own
  67.9 1.8 collective-permute-done.2.both
  69.7 2.4 collective-permute-start.10
  72.2 2.7 broadcast_select_fusion.1
  74.9 15.0 %collective-permute-start.14 = (bf16[96,8192]{1,0:T(8,128)(2,1)}, bf16[96,8192]{1,0:T(8,128)(2,1)}, u32[]{:S(2)}, u32[]{:S(2)}) collective-permute-start(bf16[96,8192]{1,0:T(8,128)(2,1)} %broadcast_select_fusion.1), channel_id=1, source_target_pairs={{0,4},{1,5},{2,6},{3,7},{4,8},{5,9},{6,10},{7,11},{8,12},{9,13},{1... | collective-permute-start | bytes 4718600 | tf_op jit(solution)/shard_map/ppermute | solution.py:169
  89.9 2.2 collective-permute-done.10.near
  92.2 2.7 broadcast_select_fusion
  94.9 13.9 %collective-permute-start.15 = (bf16[96,8192]{1,0:T(8,128)(2,1)}, bf16[96,8192]{1,0:T(8,128)(2,1)}, u32[]{:S(2)}, u32[]{:S(2)}) collective-permute-start(bf16[96,8192]{1,0:T(8,128)(2,1)} %broadcast_select_fusion), channel_id=1, source_target_pairs={{0,4},{1,5},{2,6},{3,7},{4,8},{5,9},{6,10},{7,11},{8,12},{9,13},{1... | collective-permute-start | bytes 4718600 | tf_op jit(solution)/shard_map/ppermute | solution.py:169
  108.8 2.4 collective-permute-start.11
  112.4 3.4 %collective-permute-start.12 = (bf16[96,8192]{1,0:T(8,128)(2,1)}, bf16[96,8192]{1,0:T(8,128)(2,1)}, u32[]{:S(2)}, u32[]{:S(2)}) collective-permute-start(bf16[96,8192]{1,0:T(8,128)(2,1)} %collective-permute-done.10.near), channel_id=1, source_target_pairs={{0,2},{1,3},{2,0},{3,1},{4,6},{5,7},{6,4},{7,5},{8,10},{9,11},{10,... | collective-permute-start | bytes 4718600 | tf_op jit(solution)/shard_map/ppermute | solution.py:160
  116.0 10.4 %collective-permute-done.14.own = bf16[96,8192]{1,0:T(8,128)(2,1)} collective-permute-done((bf16[96,8192]{1,0:T(8,128)(2,1)}, bf16[96,8192]{1,0:T(8,128)(2,1)}, u32[]{:S(2)}, u32[]{:S(2)}) %collective-permute-start.14) | collective-permute-done | bytes 1572896 | tf_op jit(solution)/shard_map/ppermute | solution.py:169
  126.5 2.4 collective-permute-start.16
  128.9 32.7 %collective-permute-done.15.near = bf16[96,8192]{1,0:T(8,128)(2,1)} collective-permute-done((bf16[96,8192]{1,0:T(8,128)(2,1)}, bf16[96,8192]{1,0:T(8,128)(2,1)}, u32[]{:S(2)}, u32[]{:S(2)}) %collective-permute-start.15) | collective-permute-done | bytes 1572896 | tf_op jit(solution)/shard_map/ppermute | solution.py:169
  161.6 3.4 %collective-permute-start.17 = (bf16[96,8192]{1,0:T(8,128)(2,1)}, bf16[96,8192]{1,0:T(8,128)(2,1)S(1)}, u32[]{:S(2)}, u32[]{:S(2)}) collective-permute-start(bf16[96,8192]{1,0:T(8,128)(2,1)} %collective-permute-done.15.near), channel_id=1, source_target_pairs={{0,2},{1,3},{2,0},{3,1},{4,6},{5,7},{6,4},{7,5},{8,10},{9,11},{10,... | collective-permute-start | bytes 4718600 | tf_op jit(solution)/shard_map/ppermute | solution.py:160
  166.5 11.6 %shard_map.59 = bf16[384,1024]{1,0:T(8,128)(2,1)S(1)} custom-call(s32[2]{0:T(128)S(1)} %add_convert_fusion.4.flags, bf16[96,8192]{1,0:T(8,128)(2,1)S(1)} %bitcast.42, bf16[96,8192]{1,0:T(8,128)(2,1)S(1)} %copy-done.2, bf16[96,8192]{1,0:T(8,128)(2,1)} %collective-permute-done.1.far, bf16[96,8192]{1,0:T(8,128)(2,1)} %collective-permute-done.2.both, ...), custom_call_target="tpu_custom_call" | custom-call | flops 6442450944 | bytes 23855104 | tf_op jit(solution)/shard_map/pallas_call | solution.py:125
  178.2 12.0 %shard_map.60 = bf16[384,1024]{1,0:T(8,128)(2,1)S(1)} custom-call(s32[2]{0:T(128)S(1)} %add_convert_fusion.4.flags, bf16[96,8192]{1,0:T(8,128)(2,1)} %collective-permute-done.4.own, bf16[96,8192]{1,0:T(8,128)(2,1)} %collective-permute-done.5.near, bf16[96,8192]{1,0:T(8,128)(2,1)S(1)} %copy-done.4, bf16[96,8192]{1,0:T(8,128)(2,1)} %collective-permute-done.7.both, ...), custom_call_target="tpu_custom_call" | custom-call | flops 6442450944 | bytes 23855104 | tf_op jit(solution)/shard_map/pallas_call | solution.py:125
  190.4 12.0 %shard_map.61 = bf16[384,1024]{1,0:T(8,128)(2,1)S(1)} custom-call(s32[2]{0:T(128)S(1)} %add_convert_fusion.4.flags, bf16[96,8192]{1,0:T(8,128)(2,1)S(1)} %collective-permute-done.9.own, bf16[96,8192]{1,0:T(8,128)(2,1)} %collective-permute-done.10.near, bf16[96,8192]{1,0:T(8,128)(2,1)} %collective-permute-done.11.far, ...), custom_call_target="tpu_custom_call" | custom-call | flops 6442450944 | bytes 23855104 | tf_op jit(solution)/shard_map/pallas_call | solution.py:125
  202.5 11.7 %shard_map.62 = bf16[384,1024]{1,0:T(8,128)(2,1)S(1)} custom-call(s32[2]{0:T(128)S(1)} %add_convert_fusion.4.flags, bf16[96,8192]{1,0:T(8,128)(2,1)} %collective-permute-done.14.own, bf16[96,8192]{1,0:T(8,128)(2,1)} %collective-permute-done.15.near, bf16[96,8192]{1,0:T(8,128)(2,1)S(1)} %collective-permute-done.16.far, ...), custom_call_target="tpu_custom_call" | custom-call | flops 6442450944 | bytes 23855104 | tf_op jit(solution)/shard_map/pallas_call | solution.py:125
  217.7 3.9 %convolution_convert_fusion = bf16[1536,768]{1,0:T(8,128)(2,1)} fusion(bf16[1536,1024]{1,0:T(8,128)(2,1)S(1)} %bitcast_dynamic-update-slice_fusion, s32[]{:T(128)S(6)} %select_n.120), kind=kOutput, calls=%fused_computation.1 | convolution fusion | flops 2417098752 | bytes 7077892 | tf_op jit(solution)/shard_map/dot_general | solution.py:23
  221.6 4.6 %all-to-all-start = ((bf16[16,96,768]{2,1,0:T(8,128)(2,1)}), bf16[16,96,768]{2,1,0:T(8,128)(2,1)S(1)}, u32[]{:S(2)}, u32[]{:S(2)}) async-start(bf16[16,96,768]{2,1,0:T(8,128)(2,1)} %bitcast.59), calls=%async_computation | async-start | bytes 4718592 | tf_op jit(solution)/shard_map/all_to_all | solution.py:204
  226.5 47.4 %all-to-all-done = bf16[16,96,768]{2,1,0:T(8,128)(2,1)S(1)} async-done(((bf16[16,96,768]{2,1,0:T(8,128)(2,1)}), bf16[16,96,768]{2,1,0:T(8,128)(2,1)S(1)}, u32[]{:S(2)}, u32[]{:S(2)}) %all-to-all-start) | async-done | bytes 2359328 | tf_op jit(solution)/shard_map/all_to_all | solution.py:204
  276.2 18.7 %all_to_all.10 = f32[32,8,128]{2,1,0:T(8,128)S(1)} all-to-all(f32[32,8,128]{2,1,0:T(8,128)S(1)} %broadcast_in_dim.2), channel_id=1, replica_groups=mesh['aux'=2,'pair'=16] {'aux','pair'}, dimensions={0} | all-to-all | bytes 262144 | tf_op jit(solution)/shard_map/all_to_all | solution.py:19
  (60 shorter events, 9.5 us)
Async XLA Ops:
  0.6 38.9 %collective-permute-start.4 = (bf16[96,8192]{1,0:T(8,128)(2,1)}, bf16[96,8192]{1,0:T(8,128)(2,1)}, u32[]{:S(2)}, u32[]{:S(2)}) collective-permute-start(bf16[96,8192]{1,0:T(8,128)(2,1)} %bitcast.39), channel_id=1, source_target_pairs={{0,4},{1,5},{2,6},{3,7},{4,8},{5,9},{6,10},{7,11},{8,12},{9,13},{1... | collective-permute-start | bytes 4718600 | tf_op jit(solution)/shard_map/ppermute | solution.py:169
  5.6 37.3 %collective-permute-start = (bf16[96,8192]{1,0:T(8,128)(2,1)}, bf16[96,8192]{1,0:T(8,128)(2,1)S(1)}, u32[]{:S(2)}, u32[]{:S(2)}) collective-permute-start(bf16[96,8192]{1,0:T(8,128)(2,1)} %bitcast.40), channel_id=1, source_target_pairs={{0,1},{1,0},{2,3},{3,2},{4,5},{5,4},{6,7},{7,6},{8,9},{9,8},{10,11... | collective-permute-start | bytes 4718600 | tf_op jit(solution)/shard_map/ppermute | solution.py:160
  9.0 44.2 %collective-permute-start.1 = (bf16[96,8192]{1,0:T(8,128)(2,1)}, bf16[96,8192]{1,0:T(8,128)(2,1)}, u32[]{:S(2)}, u32[]{:S(2)}) collective-permute-start(bf16[96,8192]{1,0:T(8,128)(2,1)} %bitcast.41), channel_id=1, source_target_pairs={{0,2},{1,3},{2,0},{3,1},{4,6},{5,7},{6,4},{7,5},{8,10},{9,11},{10,... | collective-permute-start | bytes 4718600 | tf_op jit(solution)/shard_map/ppermute | solution.py:160
  39.5 22.6 %collective-permute-start.5 = (bf16[96,8192]{1,0:T(8,128)(2,1)}, bf16[96,8192]{1,0:T(8,128)(2,1)}, u32[]{:S(2)}, u32[]{:S(2)}) collective-permute-start(bf16[96,8192]{1,0:T(8,128)(2,1)} %collective-permute-done.4.own), channel_id=1, source_target_pairs={{0,1},{1,0},{2,3},{3,2},{4,5},{5,4},{6,7},{7,6},{8,9},{9,8},{10,11... | collective-permute-start | bytes 4718600 | tf_op jit(solution)/shard_map/ppermute | solution.py:160
  42.9 29.3 %copy-start.1 = (bf16[96,8192]{1,0:T(8,128)(2,1)}, bf16[96,8192]{1,0:T(8,128)(2,1)S(1)}, u32[]{:S(2)}) copy-start(bf16[96,8192]{1,0:T(8,128)(2,1)S(1)} %collective-permute-done.near) | copy-start | bytes 4718596
  42.9 25.0 %collective-permute-start.9 = (bf16[96,8192]{1,0:T(8,128)(2,1)}, bf16[96,8192]{1,0:T(8,128)(2,1)S(1)}, u32[]{:S(2)}, u32[]{:S(2)}) collective-permute-start(bf16[96,8192]{1,0:T(8,128)(2,1)} %collective-permute-done.4.own), channel_id=1, source_target_pairs={{0,4},{1,5},{2,6},{3,7},{4,8},{5,9},{6,10},{7,11},{8,12},{9,13},{1... | collective-permute-start | bytes 4718600 | tf_op jit(solution)/shard_map/ppermute | solution.py:169
  47.3 22.4 %collective-permute-start.2 = (bf16[96,8192]{1,0:T(8,128)(2,1)S(1)}, bf16[96,8192]{1,0:T(8,128)(2,1)}, u32[]{:S(2)}, u32[]{:S(2)}) collective-permute-start(bf16[96,8192]{1,0:T(8,128)(2,1)S(1)} %collective-permute-done.near), channel_id=1, source_target_pairs={{0,2},{1,3},{2,0},{3,1},{4,6},{5,7},{6,4},{7,5},{8,10},{9,11},{10,... | collective-permute-start | bytes 4718600 | tf_op jit(solution)/shard_map/ppermute | solution.py:160
  50.8 60.4 %collective-permute-start.6 = (bf16[96,8192]{1,0:T(8,128)(2,1)}, bf16[96,8192]{1,0:T(8,128)(2,1)S(1)}, u32[]{:S(2)}, u32[]{:S(2)}) collective-permute-start(bf16[96,8192]{1,0:T(8,128)(2,1)} %collective-permute-done.4.own), channel_id=1, source_target_pairs={{0,2},{1,3},{2,0},{3,1},{4,6},{5,7},{6,4},{7,5},{8,10},{9,11},{10,... | collective-permute-start | bytes 4718600 | tf_op jit(solution)/shard_map/ppermute | solution.py:160
  62.1 53.9 %collective-permute-start.7 = (bf16[96,8192]{1,0:T(8,128)(2,1)}, bf16[96,8192]{1,0:T(8,128)(2,1)}, u32[]{:S(2)}, u32[]{:S(2)}) collective-permute-start(bf16[96,8192]{1,0:T(8,128)(2,1)} %collective-permute-done.5.near), channel_id=1, source_target_pairs={{0,2},{1,3},{2,0},{3,1},{4,6},{5,7},{6,4},{7,5},{8,10},{9,11},{10,... | collective-permute-start | bytes 4718600 | tf_op jit(solution)/shard_map/ppermute | solution.py:160
  69.7 22.4 %collective-permute-start.10 = (bf16[96,8192]{1,0:T(8,128)(2,1)S(1)}, bf16[96,8192]{1,0:T(8,128)(2,1)}, u32[]{:S(2)}, u32[]{:S(2)}) collective-permute-start(bf16[96,8192]{1,0:T(8,128)(2,1)S(1)} %collective-permute-done.9.own), channel_id=1, source_target_pairs={{0,1},{1,0},{2,3},{3,2},{4,5},{5,4},{6,7},{7,6},{8,9},{9,8},{10,11... | collective-permute-start | bytes 4718600 | tf_op jit(solution)/shard_map/ppermute | solution.py:160
  74.9 90.1 %copy-start = (bf16[8192,96]{0,1:T(8,128)(2,1)S(1)}, bf16[8192,96]{0,1:T(8,128)(2,1)}, u32[]{:S(2)}) copy-start(bf16[8192,96]{0,1:T(8,128)(2,1)} %param.5) | copy-start | bytes 4718596
  74.9 51.5 %collective-permute-start.14 = (bf16[96,8192]{1,0:T(8,128)(2,1)}, bf16[96,8192]{1,0:T(8,128)(2,1)}, u32[]{:S(2)}, u32[]{:S(2)}) collective-permute-start(bf16[96,8192]{1,0:T(8,128)(2,1)} %broadcast_select_fusion.1), channel_id=1, source_target_pairs={{0,4},{1,5},{2,6},{3,7},{4,8},{5,9},{6,10},{7,11},{8,12},{9,13},{1... | collective-permute-start | bytes 4718600 | tf_op jit(solution)/shard_map/ppermute | solution.py:169
  94.9 66.7 %collective-permute-start.15 = (bf16[96,8192]{1,0:T(8,128)(2,1)}, bf16[96,8192]{1,0:T(8,128)(2,1)}, u32[]{:S(2)}, u32[]{:S(2)}) collective-permute-start(bf16[96,8192]{1,0:T(8,128)(2,1)} %broadcast_select_fusion), channel_id=1, source_target_pairs={{0,4},{1,5},{2,6},{3,7},{4,8},{5,9},{6,10},{7,11},{8,12},{9,13},{1... | collective-permute-start | bytes 4718600 | tf_op jit(solution)/shard_map/ppermute | solution.py:169
  108.8 81.5 %collective-permute-start.11 = (bf16[96,8192]{1,0:T(8,128)(2,1)S(1)}, bf16[96,8192]{1,0:T(8,128)(2,1)}, u32[]{:S(2)}, u32[]{:S(2)}) collective-permute-start(bf16[96,8192]{1,0:T(8,128)(2,1)S(1)} %collective-permute-done.9.own), channel_id=1, source_target_pairs={{0,2},{1,3},{2,0},{3,1},{4,6},{5,7},{6,4},{7,5},{8,10},{9,11},{10,... | collective-permute-start | bytes 4718600 | tf_op jit(solution)/shard_map/ppermute | solution.py:160
  111.2 1.1 copy-start.3
  112.4 78.0 %collective-permute-start.12 = (bf16[96,8192]{1,0:T(8,128)(2,1)}, bf16[96,8192]{1,0:T(8,128)(2,1)}, u32[]{:S(2)}, u32[]{:S(2)}) collective-permute-start(bf16[96,8192]{1,0:T(8,128)(2,1)} %collective-permute-done.10.near), channel_id=1, source_target_pairs={{0,2},{1,3},{2,0},{3,1},{4,6},{5,7},{6,4},{7,5},{8,10},{9,11},{10,... | collective-permute-start | bytes 4718600 | tf_op jit(solution)/shard_map/ppermute | solution.py:160
  126.5 76.0 %collective-permute-start.16 = (bf16[96,8192]{1,0:T(8,128)(2,1)}, bf16[96,8192]{1,0:T(8,128)(2,1)S(1)}, u32[]{:S(2)}, u32[]{:S(2)}) collective-permute-start(bf16[96,8192]{1,0:T(8,128)(2,1)} %collective-permute-done.14.own), channel_id=1, source_target_pairs={{0,2},{1,3},{2,0},{3,1},{4,6},{5,7},{6,4},{7,5},{8,10},{9,11},{10,... | collective-permute-start | bytes 4718600 | tf_op jit(solution)/shard_map/ppermute | solution.py:160
  161.6 40.8 %collective-permute-start.17 = (bf16[96,8192]{1,0:T(8,128)(2,1)}, bf16[96,8192]{1,0:T(8,128)(2,1)S(1)}, u32[]{:S(2)}, u32[]{:S(2)}) collective-permute-start(bf16[96,8192]{1,0:T(8,128)(2,1)} %collective-permute-done.15.near), channel_id=1, source_target_pairs={{0,2},{1,3},{2,0},{3,1},{4,6},{5,7},{6,4},{7,5},{8,10},{9,11},{10,... | collective-permute-start | bytes 4718600 | tf_op jit(solution)/shard_map/ppermute | solution.py:160
  165.1 1.4 copy-start.2
  166.5 11.7 %copy-start.4 = (bf16[96,8192]{1,0:T(8,128)(2,1)S(1)}, bf16[96,8192]{1,0:T(8,128)(2,1)}, u32[]{:S(2)}) copy-start(bf16[96,8192]{1,0:T(8,128)(2,1)} %copy-done.3) | copy-start | bytes 4718596
  178.1 36.1 %collective-permute-start.3 = (bf16[384,1024]{1,0:T(8,128)(2,1)S(1)}, bf16[384,1024]{1,0:T(8,128)(2,1)S(1)}, u32[]{:S(2)}, u32[]{:S(2)}) collective-permute-start(bf16[384,1024]{1,0:T(8,128)(2,1)S(1)} %shard_map.59), channel_id=1, source_target_pairs={{0,16},{16,0},{1,17},{17,1},{2,18},{18,2},{3,19},{19,3},{4,20},{20... | collective-permute-start | bytes 2359304 | tf_op jit(solution)/shard_map/ppermute | solution.py:175
  190.3 24.3 %collective-permute-start.8 = (bf16[384,1024]{1,0:T(8,128)(2,1)S(1)}, bf16[384,1024]{1,0:T(8,128)(2,1)S(1)}, u32[]{:S(2)}, u32[]{:S(2)}) collective-permute-start(bf16[384,1024]{1,0:T(8,128)(2,1)S(1)} %shard_map.60), channel_id=1, source_target_pairs={{0,16},{16,0},{1,17},{17,1},{2,18},{18,2},{3,19},{19,3},{4,20},{20... | collective-permute-start | bytes 2359304 | tf_op jit(solution)/shard_map/ppermute | solution.py:175
  202.4 12.5 %collective-permute-start.13 = (bf16[384,1024]{1,0:T(8,128)(2,1)S(1)}, bf16[384,1024]{1,0:T(8,128)(2,1)S(1)}, u32[]{:S(2)}, u32[]{:S(2)}) collective-permute-start(bf16[384,1024]{1,0:T(8,128)(2,1)S(1)} %shard_map.61), channel_id=1, source_target_pairs={{0,16},{16,0},{1,17},{17,1},{2,18},{18,2},{3,19},{19,3},{4,20},{20... | collective-permute-start | bytes 2359304 | tf_op jit(solution)/shard_map/ppermute | solution.py:175
  214.1 2.4 collective-permute-start.18
  221.6 4.6 %copy-start.5 = (f32[768]{0:T(1024)S(1)}, f32[768]{0:T(1024)}, u32[]{:S(2)}) copy-start(f32[768]{0:T(1024)} %param.7) | copy-start | bytes 9220
  221.6 4.6 %copy-start.6 = (f32[2]{0:T(128)S(1)}, f32[2]{0:T(128)}, u32[]{:S(2)}) copy-start(f32[2]{0:T(128)} %param.6) | copy-start | bytes 28
  221.6 52.2 %all-to-all-start = ((bf16[16,96,768]{2,1,0:T(8,128)(2,1)}), bf16[16,96,768]{2,1,0:T(8,128)(2,1)S(1)}, u32[]{:S(2)}, u32[]{:S(2)}) async-start(bf16[16,96,768]{2,1,0:T(8,128)(2,1)} %bitcast.59), calls=%async_computation | async-start | bytes 4718592 | tf_op jit(solution)/shard_map/all_to_all | solution.py:204
